TPU v7x, 32 devices: a whole 2x2x4 slice. The times are simulated.
32 devices in a mesh: groups: 2 (over x), engine: 2 (over core), tp: 8 (over z, y).
Axes of the slice: x: 2, y: 2, z: 4, core: 2. Of those that a mesh axis runs over, the one named last changes fastest.
Arguments:
- tokens: bfloat16 [4096, 8192], P(('groups', 'engine'), 'tp'), parts along dimension 0, may hold values from -200 to 200
- norm_gain: float32 [8192], replicated, may hold values from 0.1 to 1.9
- qkv_weight: bfloat16 [8192, 10240], P(('engine', 'tp')), may hold values from -0.0625 to 0.0625
Outputs:
- projections: bfloat16 [4096, 10240], P(('groups', 'engine'), 'tp'), parts along dimension 0
There are 2 independent parts, one for each index of `groups`. A program takes and returns all parts, laid end to end along the dimension named above; an argument that names none is the same for every part. Nothing has to cross between parts.
All inputs are finite; a program needn't handle non-finite values.
Results may differ from a plain program's by a relative error of at most 0.0049.
Values may be sent and summed in bfloat16 or wider, within the bound.
A program may use at most 192 MiB of HBM per device.

v0:
```python
import jax
import jax.numpy as jnp
from jax import lax
from jax.sharding import PartitionSpec as P


def body(tokens, norm_gain, qkv_weight):
    whole = lax.all_gather(tokens, "tp", axis=1, tiled=True)
    widened = whole.astype(jnp.float32)
    mean_square = jnp.mean(widened * widened, axis=1, keepdims=True)
    normed = (widened * lax.rsqrt(mean_square + 1e-05) * norm_gain[None, :]).astype(jnp.bfloat16)
    engines = lax.axis_size("engine")
    tensor_ways = lax.axis_size("tp")
    row_count = qkv_weight.shape[0]
    token_rows = normed.shape[0]
    paired = lax.all_gather(qkv_weight, "engine", axis=0, tiled=True)
    dealt = lax.all_to_all(paired, "tp", split_axis=1, concat_axis=0, tiled=True)
    blocks = dealt.reshape(tensor_ways, engines, row_count, dealt.shape[1])
    features = normed.reshape(token_rows, engines, tensor_ways, row_count)
    projected = jnp.einsum("aetr,terc->ac", features, blocks, preferred_element_type=jnp.float32)
    return projected.astype(jnp.bfloat16)


def solution(mesh):
    placed = (P(("groups", "engine"), "tp"), P(), P(("engine", "tp"), None))
    return jax.shard_map(
        body, mesh=mesh, in_specs=placed, out_specs=P(("groups", "engine"), "tp"), check_vma=False
    )
```

profile of v0, /device:TPU:9, one launch (start us, length us, event | category | flops | bytes accessed | tf_op | source)
XLA Modules:
  0.0 788.4 jit_solution(2457885474768910361)
XLA Ops:
  7.4 0.0 all-gather.5.cloned.1.call-start
  7.4 14.4 %copy.7 = bf16[512,10240]{0,1:T(8,128)(2,1)} copy(bf16[512,10240]{1,0:T(8,128)(2,1)} %param.5) | data formatting | bytes 20971520 | tf_op args[2]
  21.8 0.0 all-gather.5.cloned.1.call-update
  21.8 37.9 %all-gather.5.cloned.1.call-done = bf16[1024,10240]{0,1:T(8,128)(2,1)} async-done(((bf16[512,10240]{0,1:T(8,128)(2,1)}), bf16[1024,10240]{0,1:T(8,128)(2,1)}) %all-gather.5.cloned.1.call-update) | async-done | bytes 20971536 | tf_op jit(solution)/shard_map/all_gather | solution.py:16
  59.7 6.0 all-to-all-start
  65.7 0.0 copy-start.1
  65.8 0.0 all-gather.3.cloned.1.call-start
  65.8 0.5 all-gather.3.cloned.1.call-update
  66.3 606.9 %all-gather.3.cloned.1.call-done = bf16[1024,8192]{1,0:T(8,128)(2,1)} async-done(((bf16[1024,1024]{1,0:T(8,128)(2,1)}), bf16[1024,8192]{1,0:T(8,128)(2,1)}) %all-gather.3.cloned.1.call-update) | async-done | bytes 16777232 | tf_op jit(solution)/shard_map/all_gather | solution.py:8
  673.2 0.0 copy-start
  673.2 7.5 fusion
  680.7 0.0 copy-done.1
  680.7 3.1 copy-done
  683.9 4.7 fusion.2
  688.6 10.1 %copy.12 = bf16[128,8,16,512]{3,2,1,0:T(8,128)(2,1)} copy(bf16[128,8,16,512]{3,1,2,0:T(8,128)(2,1)S(1)} %bitcast.10) | data formatting | bytes 33554432
  698.7 19.1 %all-to-all-done = bf16[1024,8,1280]{0,2,1:T(8,128)(2,1)} async-done(((bf16[1024,8,1280]{0,2,1:T(8,128)(2,1)}), bf16[1024,8,1280]{0,2,1:T(8,128)(2,1)}, u32[]{:S(2)}, u32[]{:S(2)}) %all-to-all-start) | async-done | bytes 20971552 | tf_op jit(solution)/shard_map/all_to_all | solution.py:17
  717.8 28.5 %copy.8 = bf16[8,1024,1280]{2,1,0:T(8,128)(2,1)} copy(bf16[8,1024,1280]{1,2,0:T(8,128)(2,1)} %bitcast.1) | data formatting | bytes 41943040 | tf_op jit(solution)/shard_map/all_to_all | solution.py:17
  746.4 34.6 %bitcast_convert_fusion = bf16[1024,1280]{1,0:T(8,128)(2,1)} fusion(bf16[8,2,512,1280]{3,2,1,0:T(8,128)(2,1)} %bitcast.12, bf16[1024,2,8,512]{3,2,1,0:T(8,128)(2,1)} %bitcast.13), kind=kOutput, calls=%fused_computation.8 | convolution fusion | flops 21476147200 | bytes 40370176 | tf_op jit(solution)/shard_map/aetr,terc->ac/dot_general | solution.py:20
  (1 shorter events, 0.0 us)
Async XLA Ops:
  7.4 52.3 %all-gather.5.cloned.1.call-start = ((), (), s32[]{:S(2)}) async-start(), calls=%async_computation.2 | async-start | bytes 31457280 | tf_op jit(solution)/shard_map/all_gather | solution.py:16
  59.7 658.1 %all-to-all-start = ((bf16[1024,8,1280]{0,2,1:T(8,128)(2,1)}), bf16[1024,8,1280]{0,2,1:T(8,128)(2,1)}, u32[]{:S(2)}, u32[]{:S(2)}) async-start(bf16[1024,8,1280]{0,2,1:T(8,128)(2,1)} %bitcast.11), calls=%async_computation | async-start | bytes 41943040 | tf_op jit(solution)/shard_map/all_to_all | solution.py:17
  65.7 615.0 %copy-start.1 = (f32[8192]{0:T(1024)S(1)}, f32[8192]{0:T(1024)}, u32[]{:S(2)}) copy-start(f32[8192]{0:T(1024)} %param.4) | copy-start | bytes 98308
  65.8 607.5 %all-gather.3.cloned.1.call-start = ((), (), s32[]{:S(2)}) async-start(), calls=%async_computation.1 | async-start | bytes 18874368 | tf_op jit(solution)/shard_map/all_gather | solution.py:8
  673.2 10.7 %copy-start = (bf16[1024,8192]{1,0:T(8,128)(2,1)S(1)}, bf16[1024,8192]{1,0:T(8,128)(2,1)}, u32[]{:S(2)}) copy-start(bf16[1024,8192]{1,0:T(8,128)(2,1)} %all-gather.3.cloned.1.call-done) | copy-start | bytes 50331652
Sparse Core Ops, SparseCore 0:
  21.9 37.7 all-gather.4
Sparse Core Ops, SparseCore 1:
  68.4 604.8 all-gather.2
where the time goes:
time: 794 us; the launch traced here: 788 us
  waiting for transfers between devices  664 us (84%)
  local copies, waits for them, and re-layouts  56.2 us (7%)
  matrix products  34.6 us (4%)
  between operations  14.9 us (2%)
  other arithmetic  12.2 us (2%)
    all_gather x1, waiting for transfers between devices, body(): whole = lax.all_gather(tokens, 'tp', axis=1, tiled=True)  607 us
    all_gather x1, waiting for transfers between devices, body(): paired = lax.all_gather(qkv_weight, 'engine', axis=0, tiled=True)  37.9 us
    dot_general x1, matrix products, body(): jnp.einsum('aetr,terc->ac', features, blocks, preferred_element_type=jnp....  34.6 us
    all_to_all x1, local copies, waits for them, and re-layouts, body(): lax.all_to_all(paired, 'tp', split_axis=1, concat_axis=0, tiled=True)  28.5 us
    unnamed x6, local copies, waits for them, and re-layouts  27.6 us
    all_to_all x1, waiting for transfers between devices, body(): lax.all_to_all(paired, 'tp', split_axis=1, concat_axis=0, tiled=True)  19.1 us
  transfers between devices with their start and end apart: 3, of which 3 were waited for; matrix products, arithmetic and copies ran while one was open for 3% of the time, Pallas kernels for 0%

commit v1 on v0

v1 whole, which is shorter than its diff:
```python
import functools

import jax
import jax.numpy as jnp
from jax import lax
from jax.experimental import pallas as pl
from jax.experimental.pallas import tpu as pltpu
from jax.sharding import PartitionSpec as P

MESH = pl.DeviceIdType.MESH
CHUNKS = 4
EPS = 1e-05


def plain_body(tokens, norm_gain, qkv_weight):
    whole = lax.all_gather(tokens, "tp", axis=1, tiled=True)
    widened = whole.astype(jnp.float32)
    mean_square = jnp.mean(widened * widened, axis=1, keepdims=True)
    normed = (widened * lax.rsqrt(mean_square + EPS) * norm_gain[None, :]).astype(jnp.bfloat16)
    engines = lax.axis_size("engine")
    tensor_ways = lax.axis_size("tp")
    row_count = qkv_weight.shape[0]
    token_rows = normed.shape[0]
    paired = lax.all_gather(qkv_weight, "engine", axis=0, tiled=True)
    dealt = lax.all_to_all(paired, "tp", split_axis=1, concat_axis=0, tiled=True)
    blocks = dealt.reshape(tensor_ways, engines, row_count, dealt.shape[1])
    features = normed.reshape(token_rows, engines, tensor_ways, row_count)
    projected = jnp.einsum("aetr,terc->ac", features, blocks, preferred_element_type=jnp.float32)
    return projected.astype(jnp.bfloat16)


def kernel(rows, depth, width, tok_ref, gain_ref, w_ref, out_ref,
           raw, tbuf, wbuf, pout, pin, total, obuf, squares, scale,
           load_sem, wload_sem, out_sem, send_sem, tz_sem, ty_sem, wd_sem, wx_sem, wc_sem, p_sem, s_sem):
    x = lax.axis_index("groups")
    e = lax.axis_index("engine")
    me = lax.axis_index("tp")
    y = me % 2
    z = me // 2
    zh = z // 2
    zl = z % 2
    inner = (zh + zl) % 2
    features = raw.shape[1]
    depth_all = 4 * features
    chunk = rows // CHUNKS
    part = depth // 2
    counter = [0]
    sent = []

    def tp_at(yy, zz):
        return 2 * zz + yy

    def remote(src, dst, recv, where):
        copy = pltpu.make_async_remote_copy(
            src_ref=src, dst_ref=dst, send_sem=send_sem.at[counter[0]], recv_sem=recv,
            device_id=where, device_id_type=MESH)
        counter[0] += 1
        return copy

    def send(*args):
        copy = remote(*args)
        copy.start()
        sent.append(copy)

    def landed(dst, recv):
        pltpu.make_async_remote_copy(
            src_ref=dst, dst_ref=dst, send_sem=send_sem.at[0], recv_sem=recv,
            device_id={"tp": me}, device_id_type=MESH).wait_recv()

    def crows(q):
        return pl.ds(q * chunk, chunk)

    loads = [pltpu.make_async_copy(tok_ref.at[crows(q)], raw.at[crows(q)], load_sem.at[q]) for q in range(CHUNKS)]
    for load in loads:
        load.start()
    y_other, z_near, z_far = 1 - y, z + 1 - 2 * zl, (z + 2) % 4
    peers = [(y_other, z), (y, z_near), (y_other, z_near)]

    def columns_of(yy, zz, cs):
        owner = tp_at(yy, (zz + 2) % 4 if cs == 0 else zz)
        return pl.ds(pl.multiple_of(owner * width, width), width)

    def block_rows(ee, yy, zz):
        return pl.multiple_of((ee * 4 + (zz % 2) * 2 + yy) * depth, depth)

    mine = block_rows(e, y, z)
    wloads = [
        pltpu.make_async_copy(w_ref.at[:, columns_of(y, z, cs)], wbuf.at[cs, pl.ds(mine, depth)], wload_sem.at[cs])
        for cs in range(2)
    ]
    for load in wloads:
        load.start()

    barrier = pltpu.get_barrier_semaphore()
    for d in range(1, 8):
        pl.semaphore_signal(barrier, inc=1, device_id={"tp": (me + d) % 8}, device_id_type=MESH)
    pl.semaphore_signal(barrier, inc=1, device_id={"groups": 1 - x}, device_id_type=MESH)
    pl.semaphore_signal(barrier, inc=1, device_id={"engine": 1 - e}, device_id_type=MESH)
    pl.semaphore_wait(barrier, 9)

    def send_weights(cs):
        for d, (yy, zz) in enumerate(peers):
            send(w_ref.at[pl.ds(pl.multiple_of(x * part, part), part), columns_of(yy, zz, cs)],
                 wbuf.at[cs, pl.ds(mine + x * part, part)],
                 wd_sem.at[cs * 3 + d], {"tp": tp_at(yy, zz)})
        send(w_ref.at[:, columns_of(y, z, cs)], wbuf.at[cs, pl.ds(mine, depth)],
             wc_sem.at[cs * 7 + 6], {"engine": 1 - e})

    def pass_direct(cs, d):
        region = wbuf.at[cs, pl.ds(block_rows(e, *peers[d]) + x * part, part)]
        landed(region, wd_sem.at[cs * 3 + d])
        send(region, region, wx_sem.at[cs * 3 + d], {"groups": 1 - x})
        send(region, region, wc_sem.at[cs * 7 + d], {"engine": 1 - e})

    def pass_across(cs, d):
        region = wbuf.at[cs, pl.ds(block_rows(e, *peers[d]) + (1 - x) * part, part)]
        landed(region, wx_sem.at[cs * 3 + d])
        send(region, region, wc_sem.at[cs * 7 + 3 + d], {"engine": 1 - e})

    def weights_here(cs):
        for d in range(3):
            first = block_rows(1 - e, *peers[d])
            landed(wbuf.at[cs, pl.ds(first + x * part, part)], wc_sem.at[cs * 7 + d])
            landed(wbuf.at[cs, pl.ds(first + (1 - x) * part, part)], wc_sem.at[cs * 7 + 3 + d])
        landed(wbuf.at[cs, pl.ds(block_rows(1 - e, y, z), depth)], wc_sem.at[cs * 7 + 6])
        wloads[cs].wait()

    send_weights(0)

    def tcols(index):
        return pl.ds(pl.multiple_of(index * features, features), features)

    def tslot(slot, yy, q):
        return tbuf.at[crows(q), tcols(slot * 2 + yy)]

    home, cross = zh, 1 - zh
    own_index = (1 - inner) * (home * 2 + y) + inner * 4
    gain = gain_ref[:, pl.ds(pl.multiple_of(me * features, features), features)]
    z_sends = [remote(tbuf.at[crows(q), tcols(own_index)], tslot(home, y, q), tz_sem.at[inner * CHUNKS + q],
                      {"tp": tp_at(y, z + 1 - 2 * zh)}) for q in range(CHUNKS)]
    z_passes = [remote(tslot(cross, y, q), tslot(cross, y, q), tz_sem.at[CHUNKS + q],
                       {"tp": tp_at(y, z_near)}) for q in range(CHUNKS)]
    y_home = [remote(tslot(home, y, q), tslot(home, y, q), ty_sem.at[home * CHUNKS + q],
                     {"tp": tp_at(y_other, z)}) for q in range(CHUNKS)]
    y_cross = [remote(tslot(cross, y, q), tslot(cross, y, q), ty_sem.at[cross * CHUNKS + q],
                      {"tp": tp_at(y_other, z)}) for q in range(CHUNKS)]

    for q in range(CHUNKS):
        loads[q].wait()
        tbuf[crows(q), tcols(own_index)] = (raw[crows(q)].astype(jnp.float32) * gain).astype(jnp.bfloat16)
        z_sends[q].start()
        if q < 2:
            @pl.when(inner == 0)
            def _():
                y_home[q].start()

    def pass_tokens(q):
        if q >= 2:
            @pl.when(inner == 0)
            def _():
                y_home[q].start()

        @pl.when(inner == 1)
        def _():
            landed(tslot(home, y, q), tz_sem.at[q])
            y_home[q].start()
        landed(tslot(cross, y, q), tz_sem.at[CHUNKS + q])

        @pl.when(inner == 1)
        def _():
            z_passes[q].start()
        y_cross[q].start()

    pass_tokens(0)
    pass_direct(0, 0)
    pass_direct(0, 1)
    pass_tokens(1)
    pass_direct(0, 2)
    pass_tokens(2)
    pass_tokens(3)
    send_weights(1)

    ones = jnp.ones((8, features), jnp.bfloat16)
    contract_last = (((1,), (1,)), ((), ()))
    for q in range(CHUNKS):
        wide = raw[crows(q)].astype(jnp.float32)
        square = wide * wide
        high = square.astype(jnp.bfloat16)
        low = (square - high.astype(jnp.float32)).astype(jnp.bfloat16)
        squares[me, :, crows(q)] = (
            lax.dot_general(ones, high, contract_last, preferred_element_type=jnp.float32)
            + lax.dot_general(ones, low, contract_last, preferred_element_type=jnp.float32))
    for d in range(1, 8):
        send(squares.at[me], squares.at[me], s_sem.at[d], {"tp": (me + d) % 8})
    for d in range(3):
        pass_across(0, d)
    weights_here(0)

    tile = 256

    def multiply(q, cs, put):
        @pl.loop(0, width // tile)
        def _(n):
            cols = pl.ds(pl.multiple_of(n * tile, tile), tile)
            put(cols, jnp.dot(tbuf[crows(q), pl.ds(0, depth_all)], wbuf[cs, :, cols],
                              preferred_element_type=jnp.float32))

    for q in range(CHUNKS):
        for slot in range(2):
            landed(tslot(slot, y_other, q), ty_sem.at[slot * CHUNKS + q])

        def put(cols, value):
            pout[crows(q), cols] = value.astype(jnp.bfloat16)
        multiply(q, 0, put)
        send(pout.at[crows(q)], pin.at[crows(q)], p_sem.at[q], {"tp": tp_at(y, z_far)})
        if q == 1:
            for d in range(3):
                pass_direct(1, d)
    for d in range(3):
        pass_across(1, d)
    for d in range(1, 8):
        landed(squares.at[(me + 8 - d) % 8], s_sem.at[d])
    summed = squares[0]
    for d in range(1, 8):
        summed = summed + squares[d]
    inverse = lax.rsqrt(summed / (8 * features) + EPS)
    scale[...] = jnp.broadcast_to(inverse[0:1], (128, rows)).T
    weights_here(1)
    for q in range(CHUNKS):
        def put(cols, value):
            total[crows(q), cols] = value
        multiply(q, 1, put)
    outs = []
    for q in range(CHUNKS):
        landed(pin.at[crows(q)], p_sem.at[q])
        obuf[crows(q)] = ((total[crows(q)] + pin[crows(q)].astype(jnp.float32)) * scale[crows(q), 0:1]).astype(jnp.bfloat16)
        copy = pltpu.make_async_copy(obuf.at[crows(q)], out_ref.at[crows(q)], out_sem.at[q])
        copy.start()
        outs.append(copy)
    for copy in outs:
        copy.wait()
    for copy in sent + z_sends + y_home + y_cross:
        copy.wait_send()

    @pl.when(inner == 1)
    def _():
        for copy in z_passes:
            copy.wait_send()


def body(tokens, norm_gain, qkv_weight):
    rows, features = tokens.shape
    depth, columns = qkv_weight.shape
    width = columns // 8
    dma = pltpu.SemaphoreType.DMA
    return pl.pallas_call(
        functools.partial(kernel, rows, depth, width),
        out_shape=jax.ShapeDtypeStruct((rows, width), jnp.bfloat16),
        in_specs=[
            pl.BlockSpec(memory_space=pl.ANY),
            pl.BlockSpec(memory_space=pltpu.VMEM),
            pl.BlockSpec(memory_space=pl.ANY),
        ],
        out_specs=pl.BlockSpec(memory_space=pl.ANY),
        scratch_shapes=[
            pltpu.VMEM((rows, features), jnp.bfloat16),
            pltpu.VMEM((rows, 5 * features), jnp.bfloat16),
            pltpu.VMEM((2, 8 * depth, width), jnp.bfloat16),
            pltpu.VMEM((rows, width), jnp.bfloat16),
            pltpu.VMEM((rows, width), jnp.bfloat16),
            pltpu.VMEM((rows, width), jnp.float32),
            pltpu.VMEM((rows, width), jnp.bfloat16),
            pltpu.VMEM((8, 8, rows), jnp.float32),
            pltpu.VMEM((rows, 128), jnp.float32),
            dma((CHUNKS,)), dma((2,)), dma((CHUNKS,)), dma((64,)),
            dma((2 * CHUNKS,)), dma((2 * CHUNKS,)), dma((6,)), dma((6,)), dma((14,)), dma((CHUNKS,)), dma((8,)),
        ],
        compiler_params=pltpu.CompilerParams(
            collective_id=0, has_side_effects=True, vmem_limit_bytes=58 * 1024 * 1024),
        cost_estimate=pl.CostEstimate(
            flops=2 * rows * features * 8 * width, bytes_accessed=20 * 2**20, transcendentals=0),
    )(tokens, norm_gain.reshape(1, -1), qkv_weight)


def solution(mesh):
    placed = (P(("groups", "engine"), "tp"), P(), P(("engine", "tp"), None))
    shape = mesh.shape
    fits = shape["groups"] == 2 and shape["engine"] == 2 and shape["tp"] == 8
    return jax.shard_map(
        body if fits else plain_body, mesh=mesh, in_specs=placed,
        out_specs=P(("groups", "engine"), "tp"), check_vma=False)
```

time: 794 us -> 231 us (0.29)
  waiting for transfers between devices: 664 us -> 0 us
  Pallas kernels: 0 us -> 228 us
  local copies, waits for them, and re-layouts: 56.2 us -> 3.4 us
  matrix products: 34.6 us -> 0 us
  between operations: 14.9 us -> 0.01 us
  other arithmetic: 12.2 us -> 0 us
    all_gather x2 -> x0, waiting for transfers between devices: 645 us -> none  [the longest x1 607 us: body(): whole = lax.all_gather(tokens, 'tp', axis=1, tiled=True)]
    pallas_call x0 -> x1, Pallas kernels: none -> 228 us  [body(): pl.pallas_call(functools.partial(kernel, rows, depth, width), out_shape=j...]
    dot_general x1 -> x0, matrix products: 34.6 us -> none  [body(): jnp.einsum('aetr,terc->ac', features, blocks, preferred_element_type=jnp....]
    all_to_all x1 -> x0, local copies, waits for them, and re-layouts: 28.5 us -> none  [body(): lax.all_to_all(paired, 'tp', split_axis=1, concat_axis=0, tiled=True)]
    unnamed x6 -> x1, local copies, waits for them, and re-layouts: 27.6 us -> 3.4 us
    all_to_all x1 -> x0, waiting for transfers between devices: 19.1 us -> none  [body(): lax.all_to_all(paired, 'tp', split_axis=1, concat_axis=0, tiled=True)]
  transfers between devices with their start and end apart: 3 -> 0, of which waited for: 3 -> 0; matrix products, arithmetic and copies ran while one was open for 3% -> 0% of each run, Pallas kernels for 0% -> 0%
where the time goes in v1:
time: 231 us
  Pallas kernels  228 us (99%)
  local copies, waits for them, and re-layouts  3.4 us (1%)
    pallas_call x1, Pallas kernels, body(): pl.pallas_call(functools.partial(kernel, rows, depth, width), out_shape=j...  228 us

profile of v1, /device:TPU:9, one launch (start us, length us, event | category | flops | bytes accessed | tf_op | source)
XLA Modules:
  0.0 231.0 jit_solution(1119252069792382245)
XLA Ops:
  0.0 227.6 %shard_map.37 = bf16[1024,1280]{1,0:T(8,128)(2,1)} custom-call(bf16[1024,1024]{1,0:T(8,128)(2,1)} %tok_ref.1, f32[1,8192]{1,0:T(1,128)} %bitcast.1, bf16[512,10240]{1,0:T(8,128)(2,1)} %w_ref.1), custom_call_target="tpu_custom_call" | custom-call | flops 21474836480 | bytes 20971520 | tf_op jit(solution)/shard_map/pallas_call | solution.py:256
  227.6 3.4 %copy.5 = bf16[1024,1280]{1,0:T(8,128)(2,1)} copy(bf16[1024,1280]{1,0:T(8,128)(2,1)} %shard_map.37) | data formatting | bytes 5242880

commit v2 on v1

--- a/solution.py
+++ b/solution.py
@@ -9,6 +9,11 @@
 
 MESH = pl.DeviceIdType.MESH
 CHUNKS = 4
+PIECES = 8
+AHEAD = 8
+SPLIT = 2
+DIRECT_AT = 2
+ORDER = ("t0", "t1", "d0", "d1", "t2", "t3", "d2", "t4", "t5", "t6", "t7", "w1", "x0", "x1", "x2")
 EPS = 1e-05
 
 
@@ -70,15 +75,20 @@
     def crows(q):
         return pl.ds(q * chunk, chunk)
 
-    loads = [pltpu.make_async_copy(tok_ref.at[crows(q)], raw.at[crows(q)], load_sem.at[q]) for q in range(CHUNKS)]
+    def trows(q):
+        return pl.ds(q * (rows // PIECES), rows // PIECES)
+
+    loads = [pltpu.make_async_copy(tok_ref.at[trows(q)], raw.at[trows(q)], load_sem.at[q]) for q in range(PIECES)]
     for load in loads:
         load.start()
     y_other, z_near, z_far = 1 - y, z + 1 - 2 * zl, (z + 2) % 4
     peers = [(y_other, z), (y, z_near), (y_other, z_near)]
 
-    def columns_of(yy, zz, cs):
+    span = width // SPLIT
+
+    def columns_of(yy, zz, cs, first=0, count=width):
         owner = tp_at(yy, (zz + 2) % 4 if cs == 0 else zz)
-        return pl.ds(pl.multiple_of(owner * width, width), width)
+        return pl.ds(pl.multiple_of(owner * width + first, 128), count)
 
     def block_rows(ee, yy, zz):
         return pl.multiple_of((ee * 4 + (zz % 2) * 2 + yy) * depth, depth)
@@ -98,31 +108,35 @@
     pl.semaphore_signal(barrier, inc=1, device_id={"engine": 1 - e}, device_id_type=MESH)
     pl.semaphore_wait(barrier, 9)
 
+    def piece(cs, ee, d, half):
+        h, d = divmod(d, 3)
+        return wbuf.at[cs, pl.ds(block_rows(ee, *peers[d]) + half * part, part), pl.ds(h * span, span)]
+
     def send_weights(cs):
-        for d, (yy, zz) in enumerate(peers):
-            send(w_ref.at[pl.ds(pl.multiple_of(x * part, part), part), columns_of(yy, zz, cs)],
-                 wbuf.at[cs, pl.ds(mine + x * part, part)],
-                 wd_sem.at[cs * 3 + d], {"tp": tp_at(yy, zz)})
+        for d in range(3 * SPLIT):
+            h, (yy, zz) = d // 3, peers[d % 3]
+            send(w_ref.at[pl.ds(pl.multiple_of(x * part, part), part), columns_of(yy, zz, cs, h * span, span)],
+                 wbuf.at[cs, pl.ds(mine + x * part, part), pl.ds(h * span, span)],
+                 wd_sem.at[cs * 3 * SPLIT + d], {"tp": tp_at(yy, zz)})
         send(w_ref.at[:, columns_of(y, z, cs)], wbuf.at[cs, pl.ds(mine, depth)],
-             wc_sem.at[cs * 7 + 6], {"engine": 1 - e})
+             wc_sem.at[12 * SPLIT + cs], {"engine": 1 - e})
 
     def pass_direct(cs, d):
-        region = wbuf.at[cs, pl.ds(block_rows(e, *peers[d]) + x * part, part)]
-        landed(region, wd_sem.at[cs * 3 + d])
-        send(region, region, wx_sem.at[cs * 3 + d], {"groups": 1 - x})
-        send(region, region, wc_sem.at[cs * 7 + d], {"engine": 1 - e})
+        region = piece(cs, e, d, x)
+        landed(region, wd_sem.at[cs * 3 * SPLIT + d])
+        send(region, region, wx_sem.at[cs * 3 * SPLIT + d], {"groups": 1 - x})
+        send(region, region, wc_sem.at[cs * 6 * SPLIT + d], {"engine": 1 - e})
 
     def pass_across(cs, d):
-        region = wbuf.at[cs, pl.ds(block_rows(e, *peers[d]) + (1 - x) * part, part)]
-        landed(region, wx_sem.at[cs * 3 + d])
-        send(region, region, wc_sem.at[cs * 7 + 3 + d], {"engine": 1 - e})
+        region = piece(cs, e, d, 1 - x)
+        landed(region, wx_sem.at[cs * 3 * SPLIT + d])
+        send(region, region, wc_sem.at[(cs * 2 + 1) * 3 * SPLIT + d], {"engine": 1 - e})
 
     def weights_here(cs):
-        for d in range(3):
-            first = block_rows(1 - e, *peers[d])
-            landed(wbuf.at[cs, pl.ds(first + x * part, part)], wc_sem.at[cs * 7 + d])
-            landed(wbuf.at[cs, pl.ds(first + (1 - x) * part, part)], wc_sem.at[cs * 7 + 3 + d])
-        landed(wbuf.at[cs, pl.ds(block_rows(1 - e, y, z), depth)], wc_sem.at[cs * 7 + 6])
+        for d in range(3 * SPLIT):
+            landed(piece(cs, 1 - e, d, x), wc_sem.at[cs * 6 * SPLIT + d])
+            landed(piece(cs, 1 - e, d, 1 - x), wc_sem.at[(cs * 2 + 1) * 3 * SPLIT + d])
+        landed(wbuf.at[cs, pl.ds(block_rows(1 - e, y, z), depth)], wc_sem.at[12 * SPLIT + cs])
         wloads[cs].wait()
 
     send_weights(0)
@@ -131,54 +145,56 @@
         return pl.ds(pl.multiple_of(index * features, features), features)
 
     def tslot(slot, yy, q):
-        return tbuf.at[crows(q), tcols(slot * 2 + yy)]
+        return tbuf.at[trows(q), tcols(slot * 2 + yy)]
 
     home, cross = zh, 1 - zh
     own_index = (1 - inner) * (home * 2 + y) + inner * 4
     gain = gain_ref[:, pl.ds(pl.multiple_of(me * features, features), features)]
-    z_sends = [remote(tbuf.at[crows(q), tcols(own_index)], tslot(home, y, q), tz_sem.at[inner * CHUNKS + q],
-                      {"tp": tp_at(y, z + 1 - 2 * zh)}) for q in range(CHUNKS)]
-    z_passes = [remote(tslot(cross, y, q), tslot(cross, y, q), tz_sem.at[CHUNKS + q],
-                       {"tp": tp_at(y, z_near)}) for q in range(CHUNKS)]
-    y_home = [remote(tslot(home, y, q), tslot(home, y, q), ty_sem.at[home * CHUNKS + q],
-                     {"tp": tp_at(y_other, z)}) for q in range(CHUNKS)]
-    y_cross = [remote(tslot(cross, y, q), tslot(cross, y, q), ty_sem.at[cross * CHUNKS + q],
-                      {"tp": tp_at(y_other, z)}) for q in range(CHUNKS)]
-
-    for q in range(CHUNKS):
+    z_sends = [remote(tbuf.at[trows(q), tcols(own_index)], tslot(home, y, q), tz_sem.at[inner * PIECES + q],
+                      {"tp": tp_at(y, z + 1 - 2 * zh)}) for q in range(PIECES)]
+    z_passes = [remote(tslot(cross, y, q), tslot(cross, y, q), tz_sem.at[PIECES + q],
+                       {"tp": tp_at(y, z_near)}) for q in range(PIECES)]
+    y_home = [remote(tslot(home, y, q), tslot(home, y, q), ty_sem.at[home * PIECES + q],
+                     {"tp": tp_at(y_other, z)}) for q in range(PIECES)]
+    y_cross = [remote(tslot(cross, y, q), tslot(cross, y, q), ty_sem.at[cross * PIECES + q],
+                      {"tp": tp_at(y_other, z)}) for q in range(PIECES)]
+
+    def send_tokens(q):
+        z_sends[q].start()
+
+        @pl.when(inner == 0)
+        def _():
+            y_home[q].start()
+
+    for q in range(PIECES):
         loads[q].wait()
-        tbuf[crows(q), tcols(own_index)] = (raw[crows(q)].astype(jnp.float32) * gain).astype(jnp.bfloat16)
-        z_sends[q].start()
-        if q < 2:
-            @pl.when(inner == 0)
-            def _():
-                y_home[q].start()
+        tbuf[trows(q), tcols(own_index)] = (raw[trows(q)].astype(jnp.float32) * gain).astype(jnp.bfloat16)
+        if q < AHEAD:
+            send_tokens(q)
 
     def pass_tokens(q):
-        if q >= 2:
-            @pl.when(inner == 0)
-            def _():
-                y_home[q].start()
-
         @pl.when(inner == 1)
         def _():
             landed(tslot(home, y, q), tz_sem.at[q])
             y_home[q].start()
-        landed(tslot(cross, y, q), tz_sem.at[CHUNKS + q])
+        landed(tslot(cross, y, q), tz_sem.at[PIECES + q])
 
         @pl.when(inner == 1)
         def _():
             z_passes[q].start()
         y_cross[q].start()
-
-    pass_tokens(0)
-    pass_direct(0, 0)
-    pass_direct(0, 1)
-    pass_tokens(1)
-    pass_direct(0, 2)
-    pass_tokens(2)
-    pass_tokens(3)
-    send_weights(1)
+        if q + AHEAD < PIECES:
+            send_tokens(q + AHEAD)
+
+    for step in ORDER:
+        kind, index = step[0], int(step[1])
+        if kind == "t":
+            pass_tokens(index)
+        elif kind == "w":
+            send_weights(index)
+        else:
+            for h in range(SPLIT):
+                (pass_direct if kind == "d" else pass_across)(0, h * 3 + index)
 
     ones = jnp.ones((8, features), jnp.bfloat16)
     contract_last = (((1,), (1,)), ((), ()))
@@ -192,8 +208,6 @@
             + lax.dot_general(ones, low, contract_last, preferred_element_type=jnp.float32))
     for d in range(1, 8):
         send(squares.at[me], squares.at[me], s_sem.at[d], {"tp": (me + d) % 8})
-    for d in range(3):
-        pass_across(0, d)
     weights_here(0)
 
     tile = 256
@@ -207,16 +221,17 @@
 
     for q in range(CHUNKS):
         for slot in range(2):
-            landed(tslot(slot, y_other, q), ty_sem.at[slot * CHUNKS + q])
+            for t in range(q * PIECES // CHUNKS, (q + 1) * PIECES // CHUNKS):
+                landed(tslot(slot, y_other, t), ty_sem.at[slot * PIECES + t])
 
         def put(cols, value):
             pout[crows(q), cols] = value.astype(jnp.bfloat16)
         multiply(q, 0, put)
         send(pout.at[crows(q)], pin.at[crows(q)], p_sem.at[q], {"tp": tp_at(y, z_far)})
-        if q == 1:
-            for d in range(3):
+        if q == DIRECT_AT:
+            for d in range(3 * SPLIT):
                 pass_direct(1, d)
-    for d in range(3):
+    for d in range(3 * SPLIT):
         pass_across(1, d)
     for d in range(1, 8):
         landed(squares.at[(me + 8 - d) % 8], s_sem.at[d])
@@ -272,8 +287,8 @@
             pltpu.VMEM((rows, width), jnp.bfloat16),
             pltpu.VMEM((8, 8, rows), jnp.float32),
             pltpu.VMEM((rows, 128), jnp.float32),
-            dma((CHUNKS,)), dma((2,)), dma((CHUNKS,)), dma((64,)),
-            dma((2 * CHUNKS,)), dma((2 * CHUNKS,)), dma((6,)), dma((6,)), dma((14,)), dma((CHUNKS,)), dma((8,)),
+            dma((PIECES,)), dma((2,)), dma((CHUNKS,)), dma((4 * PIECES + 24 * SPLIT + 13,)),
+            dma((2 * PIECES,)), dma((2 * PIECES,)), dma((6 * SPLIT,)), dma((6 * SPLIT,)), dma((12 * SPLIT + 2,)), dma((CHUNKS,)), dma((8,)),
         ],
         compiler_params=pltpu.CompilerParams(
             collective_id=0, has_side_effects=True, vmem_limit_bytes=58 * 1024 * 1024),

time: 231 us -> 219 us (0.948)
  Pallas kernels: 228 us -> 215 us
    pallas_call x1, Pallas kernels: 228 us -> 215 us  [body(): pl.pallas_call(functools.partial(kernel, rows, depth, width), out_shape=j...]
where the time goes in v2:
time: 219 us
  Pallas kernels  215 us (98%)
  local copies, waits for them, and re-layouts  3.4 us (2%)
    pallas_call x1, Pallas kernels, body(): pl.pallas_call(functools.partial(kernel, rows, depth, width), out_shape=j...  215 us

profile of v2, /device:TPU:9, one launch (start us, length us, event | category | flops | bytes accessed | tf_op | source)
XLA Modules:
  0.0 218.6 jit_solution(11169174217908490690)
XLA Ops:
  0.0 215.2 %shard_map.37 = bf16[1024,1280]{1,0:T(8,128)(2,1)} custom-call(bf16[1024,1024]{1,0:T(8,128)(2,1)} %tok_ref.1, f32[1,8192]{1,0:T(1,128)} %bitcast.1, bf16[512,10240]{1,0:T(8,128)(2,1)} %w_ref.1), custom_call_target="tpu_custom_call" | custom-call | flops 21474836480 | bytes 20971520 | tf_op jit(solution)/shard_map/pallas_call | solution.py:271
  215.2 3.4 %copy.5 = bf16[1024,1280]{1,0:T(8,128)(2,1)} copy(bf16[1024,1280]{1,0:T(8,128)(2,1)} %shard_map.37) | data formatting | bytes 5242880
